TPU v7x, 32 devices: a whole 2x2x4 slice. The times are simulated.
32 devices in a mesh: dp: 2 (over x), layer: 4 (over y, core), feat: 4 (over z).
Axes of the slice: x: 2, y: 2, z: 4, core: 2. Of those that a mesh axis runs over, the one named last changes fastest.
Arguments:
- resid: bfloat16 [4, 1024, 2304], P('layer', 'dp'), may hold values from -6 to 6
- enc_weight: bfloat16 [4, 2304, 2048], P('layer', None, 'feat'), may hold values from -0.125 to 0.125
- enc_bias: float32 [4, 2048], P('layer', 'feat'), may hold values from -3 to 3
- dec_weight: bfloat16 [4, 4, 2048, 2304], P('layer', None, 'feat', 'dp'), may hold values from -0.1875 to 0.1875
- dec_bias: float32 [4, 2304], P('layer', ('dp', 'feat')), may hold values from -3 to 3
- lengths: int32 [8], P('dp'), may hold values from 32 to 128, as said below
Outputs:
- recon: bfloat16 [4, 1024, 2304], P('layer', None, ('dp', 'feat'))
Inputs may be any that keep to these rules, and one draw needn't show every extreme that they name: `lengths`: the first sequence has length 128.
All inputs are finite; a program needn't handle non-finite values.
Results may differ from a plain program's by a relative error of at most 0.0047.
Values may be sent and summed in bfloat16 or wider, within the bound.
A program may use at most 64 MiB of HBM per device.

v0:
```python
import jax
import jax.numpy as jnp
from jax import lax
from jax.sharding import PartitionSpec as P

SEQ = 128


def passed_along(array, axis, by):
    size = lax.axis_size(axis)
    pairs = [(i, i + by) for i in range(size) if 0 <= i + by < size]
    return lax.ppermute(array, axis, pairs)


def per_device(resid, enc_weight, enc_bias, dec_weight, dec_bias, lengths):
    valid = (jnp.arange(SEQ)[None, :] < lengths[:, None]).reshape(-1).astype(jnp.float32)
    pre = jnp.dot(resid[0], enc_weight[0], preferred_element_type=jnp.float32) + enc_bias[0]
    acts = (jax.nn.relu(pre) * valid[:, None]).astype(jnp.bfloat16)
    target = lax.axis_index("layer")
    decoders = dec_weight[0]
    all_rows = lax.all_gather(acts, "dp", axis=0, tiled=True)
    initial = jnp.zeros((all_rows.shape[0], decoders.shape[2]), jnp.float32)
    pieces = None
    pieces = [(all_rows, target)]
    current = all_rows
    for step in range(1, lax.axis_size("layer")):
        current = passed_along(current, "layer", 1)
        pieces.append((current, target - step))
    total = initial
    for block, source in pieces:

        def apply_dec(carry):
            matrix = lax.dynamic_index_in_dim(decoders, jnp.maximum(source, 0), 0, keepdims=False)
            return carry + jnp.dot(block, matrix, preferred_element_type=jnp.float32)

        total = lax.cond((source >= 0) & (source <= target), apply_dec, lambda carry: carry, total)
    summed = lax.psum_scatter(total, "feat", scatter_dimension=1, tiled=True)
    return (summed + dec_bias[0][None, :]).astype(jnp.bfloat16)[None]


def solution(mesh):
    in_specs = (
        P("layer", "dp", None),
        P("layer", None, "feat"),
        P("layer", "feat"),
        P("layer", None, "feat", "dp"),
        P("layer", ("dp", "feat")),
        P("dp"),
    )
    out_specs = P("layer", None, ("dp", "feat"))
    return jax.shard_map(
        per_device, mesh=mesh, in_specs=in_specs, out_specs=out_specs, check_vma=False
    )
```

profile of v0, /device:TPU:4, one launch (start us, length us, event | category | flops | bytes accessed | tf_op | source)
XLA Modules:
  0.0 182.1 jit_solution(6016805285564381379)
XLA Ops:
  6.5 0.0 copy-start
  6.5 0.0 all-gather.2.cloned.1.call-start
  6.5 0.9 convert_bitcast_fusion
  7.4 0.8 copy-done
  8.2 3.8 %fusion.30 = bf16[512,512]{1,0:T(8,128)(2,1)} fusion(bf16[1,2304,512]{2,1,0:T(8,128)(2,1)S(1)} %copy-done, bf16[1,512,2304]{2,1,0:T(8,128)(2,1)} %param.14, f32[512]{0:T(512)S(1)} %convert_bitcast_fusion, f32[512]{0:T(512)} %bitcast.56), kind=kOutput, calls=%fused_computation.22 | convolution fusion | flops 1209008128 | bytes 5246976 | tf_op jit(solution)/shard_map/dot_general | solution.py:17
  12.1 0.0 all-gather.2.cloned.1.call-update
  12.1 0.0 reduce-scatter.2.cloned.1.call-start
  12.1 22.6 %all-gather.2.cloned.1.call-done = bf16[1024,512]{1,0:T(8,128)(2,1)} async-done(((bf16[512,512]{1,0:T(8,128)(2,1)}), bf16[1024,512]{1,0:T(8,128)(2,1)}) %all-gather.2.cloned.1.call-update) | async-done | bytes 1048592 | tf_op jit(solution)/shard_map/all_gather | solution.py:21
  34.8 1.9 %collective-permute-start = (bf16[1024,512]{1,0:T(8,128)(2,1)}, bf16[1024,512]{1,0:T(8,128)(2,1)S(1)}, u32[]{:S(2)}, u32[]{:S(2)}) collective-permute-start(bf16[1024,512]{1,0:T(8,128)(2,1)} %all-gather.2.cloned.1.call-done), channel_id=1, source_target_pairs={{0,4},{4,8},{8,12},{1,5},{5,9},{9,13},{2,6},{6,10},{10,14},{3,7},{... | collective-permute-start | bytes 3145736 | tf_op jit(solution)/shard_map/ppermute | solution.py:12
  36.7 14.4 %collective-permute-done = bf16[1024,512]{1,0:T(8,128)(2,1)S(1)} collective-permute-done((bf16[1024,512]{1,0:T(8,128)(2,1)}, bf16[1024,512]{1,0:T(8,128)(2,1)S(1)}, u32[]{:S(2)}, u32[]{:S(2)}) %collective-permute-start) | collective-permute-done | bytes 1048608 | tf_op jit(solution)/shard_map/ppermute | solution.py:12
  51.1 0.0 copy-start.1
  51.1 1.9 %collective-permute-start.1 = (bf16[1024,512]{1,0:T(8,128)(2,1)S(1)}, bf16[1024,512]{1,0:T(8,128)(2,1)}, u32[]{:S(2)}, u32[]{:S(2)}) collective-permute-start(bf16[1024,512]{1,0:T(8,128)(2,1)S(1)} %collective-permute-done), channel_id=1, source_target_pairs={{0,4},{4,8},{8,12},{1,5},{5,9},{9,13},{2,6},{6,10},{10,14},{3,7},{... | collective-permute-start | bytes 3145736 | tf_op jit(solution)/shard_map/ppermute | solution.py:12
  53.0 0.0 copy-done.1
  53.0 14.3 %collective-permute-done.1 = bf16[1024,512]{1,0:T(8,128)(2,1)} collective-permute-done((bf16[1024,512]{1,0:T(8,128)(2,1)S(1)}, bf16[1024,512]{1,0:T(8,128)(2,1)}, u32[]{:S(2)}, u32[]{:S(2)}) %collective-permute-start.1) | collective-permute-done | bytes 1048608 | tf_op jit(solution)/shard_map/ppermute | solution.py:12
  67.3 1.9 %collective-permute-start.2 = (bf16[1024,512]{1,0:T(8,128)(2,1)}, bf16[1024,512]{1,0:T(8,128)(2,1)S(1)}, u32[]{:S(2)}, u32[]{:S(2)}) collective-permute-start(bf16[1024,512]{1,0:T(8,128)(2,1)} %collective-permute-done.1), channel_id=1, source_target_pairs={{0,4},{4,8},{8,12},{1,5},{5,9},{9,13},{2,6},{6,10},{10,14},{3,7},{... | collective-permute-start | bytes 3145736 | tf_op jit(solution)/shard_map/ppermute | solution.py:12
  69.2 5.2 %conditional.4 = (f32[1024,1152]{0,1:T(8,128)}) conditional(s32[]{:T(128)} %convert_element_type.31, () %tuple.29, (s32[]{:T(128)}, bf16[4,512,1152]{2,1,0:T(8,128)(2,1)}, bf16[1024,512]{1,0:T(8,128)(2,1)}) %tuple.46), branch_computations={%region_0.1_spmd, %region_1.2_spmd} | conditional | flops 1207959552 | bytes 6946840 | solution.py:36
  69.2 5.2 %convolution_bitcast_fusion = f32[1024,1152]{0,1:T(8,128)} fusion(bf16[1024,512]{1,0:T(8,128)(2,1)} %get-tuple-element.52, bf16[4,512,1152]{2,1,0:T(8,128)(2,1)} %get-tuple-element.50, s32[]{:T(128)S(6)} %max.14), kind=kOutput, calls=%fused_computation | convolution fusion | flops 1207959552 | bytes 6946820 | tf_op jit(solution)/shard_map/cond/branch_1_fun/dot_general | solution.py:34
  74.4 6.6 %conditional.5 = (f32[1024,1152]{0,1:T(8,128)}) conditional(s32[]{:T(128)} %convert_element_type.30, f32[1024,1152]{0,1:T(8,128)} %get-tuple-element.65, (s32[]{:T(128)}, bf16[4,512,1152]{2,1,0:T(8,128)(2,1)}, bf16[1024,512]{1,0:T(8,128)(2,1)}, f32[1024,1152]{0,1:T(8,128)}) %tuple.50), branch_computations={%region_2.3_spmd, %region_3.4_spmd} | conditional | flops 1209139200 | bytes 11665432 | solution.py:36
  74.4 6.6 %bitcast_add_fusion = f32[1024,1152]{0,1:T(8,128)} fusion(f32[1024,1152]{0,1:T(8,128)} %get-tuple-element.53, bf16[1024,512]{1,0:T(8,128)(2,1)} %get-tuple-element.56, bf16[4,512,1152]{2,1,0:T(8,128)(2,1)} %get-tuple-element.54, s32[]{:T(128)S(6)} %max.15), kind=kOutput, calls=%fused_computation.4 | convolution fusion | flops 1209139200 | bytes 11665412 | tf_op jit(solution)/shard_map/cond/branch_1_fun/dot_general | solution.py:34
  81.0 6.6 %conditional.6 = (f32[1024,1152]{0,1:T(8,128)}) conditional(s32[]{:T(128)} %convert_element_type.29, f32[1024,1152]{0,1:T(8,128)} %get-tuple-element.66, (s32[]{:T(128)}, bf16[4,512,1152]{2,1,0:T(8,128)(2,1)}, bf16[1024,512]{1,0:T(8,128)(2,1)}, f32[1024,1152]{0,1:T(8,128)}) %tuple.48), branch_computations={%region_4.5_spmd, %region_5.6_spmd} | conditional | flops 1209139200 | bytes 11665432 | solution.py:36
  81.0 6.6 %bitcast_add_fusion.1 = f32[1024,1152]{0,1:T(8,128)} fusion(f32[1024,1152]{0,1:T(8,128)} %get-tuple-element.57, bf16[1024,512]{1,0:T(8,128)(2,1)} %get-tuple-element.60, bf16[4,512,1152]{2,1,0:T(8,128)(2,1)} %get-tuple-element.58, s32[]{:T(128)S(6)} %max.16), kind=kOutput, calls=%fused_computation.8 | convolution fusion | flops 1209139200 | bytes 11665412 | tf_op jit(solution)/shard_map/cond/branch_1_fun/dot_general | solution.py:34
  87.6 0.0 collective-permute-done.2
  87.6 0.0 copy-start.2
  87.6 0.0 reduce-scatter.2.cloned.1.call-update
  87.6 0.7 copy-done.2
  88.3 84.8 %reduce-scatter.2.cloned.1.call-done = f32[1024,288]{0,1:T(8,128)} async-done(((f32[1024,1152]{0,1:T(8,128)}), f32[1024,288]{0,1:T(8,128)}) %reduce-scatter.2.cloned.1.call-update) | async-done | bytes 1179664 | tf_op jit(solution)/shard_map/reduce_scatter | solution.py:37
  173.0 2.2 %fusion.35 = bf16[1,1024,288]{1,2,0:T(8,128)(2,1)} fusion(f32[1024,288]{0,1:T(8,128)} %reduce-scatter.2.cloned.1.call-done, f32[288]{0:T(512)S(1)} %reduce), kind=kLoop, calls=%fused_computation.24 | loop fusion | flops 589824 | bytes 1770624 | tf_op jit(solution)/shard_map/broadcast_in_dim | solution.py:38
  (2 shorter events, 0.0 us)
Async XLA Ops:
  6.5 1.7 copy-start
  6.5 28.2 %all-gather.2.cloned.1.call-start = ((), (), s32[]{:S(2)}) async-start(), calls=%async_computation.1 | async-start | bytes 1572864 | tf_op jit(solution)/shard_map/all_gather | solution.py:21
  12.1 161.0 %reduce-scatter.2.cloned.1.call-start = ((), (), s32[]{:S(2)}) async-start(), calls=%async_computation.2 | async-start | bytes 5898240 | tf_op jit(solution)/shard_map/reduce_scatter | solution.py:37
  34.8 16.3 %collective-permute-start = (bf16[1024,512]{1,0:T(8,128)(2,1)}, bf16[1024,512]{1,0:T(8,128)(2,1)S(1)}, u32[]{:S(2)}, u32[]{:S(2)}) collective-permute-start(bf16[1024,512]{1,0:T(8,128)(2,1)} %all-gather.2.cloned.1.call-done), channel_id=1, source_target_pairs={{0,4},{4,8},{8,12},{1,5},{5,9},{9,13},{2,6},{6,10},{10,14},{3,7},{... | collective-permute-start | bytes 3145736 | tf_op jit(solution)/shard_map/ppermute | solution.py:12
  51.1 1.9 %copy-start.1 = (bf16[1024,512]{1,0:T(8,128)(2,1)}, bf16[1024,512]{1,0:T(8,128)(2,1)S(1)}, u32[]{:S(2)}) copy-start(bf16[1024,512]{1,0:T(8,128)(2,1)S(1)} %collective-permute-done) | copy-start | bytes 3145732
  51.1 16.2 %collective-permute-start.1 = (bf16[1024,512]{1,0:T(8,128)(2,1)S(1)}, bf16[1024,512]{1,0:T(8,128)(2,1)}, u32[]{:S(2)}, u32[]{:S(2)}) collective-permute-start(bf16[1024,512]{1,0:T(8,128)(2,1)S(1)} %collective-permute-done), channel_id=1, source_target_pairs={{0,4},{4,8},{8,12},{1,5},{5,9},{9,13},{2,6},{6,10},{10,14},{3,7},{... | collective-permute-start | bytes 3145736 | tf_op jit(solution)/shard_map/ppermute | solution.py:12
  67.3 20.3 %collective-permute-start.2 = (bf16[1024,512]{1,0:T(8,128)(2,1)}, bf16[1024,512]{1,0:T(8,128)(2,1)S(1)}, u32[]{:S(2)}, u32[]{:S(2)}) collective-permute-start(bf16[1024,512]{1,0:T(8,128)(2,1)} %collective-permute-done.1), channel_id=1, source_target_pairs={{0,4},{4,8},{8,12},{1,5},{5,9},{9,13},{2,6},{6,10},{10,14},{3,7},{... | collective-permute-start | bytes 3145736 | tf_op jit(solution)/shard_map/ppermute | solution.py:12
  87.6 0.7 copy-start.2
Sparse Core Ops, SparseCore 0:
  12.2 22.4 all-gather.1
  87.7 85.2 reduce-scatter.1
where the time goes:
time: 184 us; the launch traced here: 182 us
  waiting for transfers between devices  136 us (74%)
  matrix products  22.2 us (12%)
  between operations  13.5 us (7%)
  starting transfers between devices  5.77 us (3%)
  other arithmetic  3.11 us (2%)
    reduce_scatter x1, waiting for transfers between devices, per_device(): summed = lax.psum_scatter(total, 'feat', scatter_dimension=1, tiled=True)  84.8 us
    ppermute x3, waiting for transfers between devices, passed_along(): return lax.ppermute(array, axis, pairs)  28.7 us
    all_gather x1, waiting for transfers between devices, per_device(): all_rows = lax.all_gather(acts, 'dp', axis=0, tiled=True)  22.6 us
    dot_general x3, matrix products, apply_dec(): return carry + jnp.dot(block, matrix, preferred_element_type=jnp.float32)  18.3 us
    ppermute x3, starting transfers between devices, passed_along(): return lax.ppermute(array, axis, pairs)  5.73 us
    dot_general x1, matrix products, per_device(): jnp.dot(resid[0], enc_weight[0], preferred_element_type=jnp.float32)  3.84 us
  transfers between devices with their start and end apart: 5, of which 4 were waited for; matrix products, arithmetic and copies ran while one was open for 10% of the time, Pallas kernels for 0%

commit v1 on v0

--- a/solution.py
+++ b/solution.py
@@ -1,9 +1,15 @@
+import functools
+
 import jax
 import jax.numpy as jnp
 from jax import lax
+from jax.experimental import pallas as pl
+from jax.experimental.pallas import tpu as pltpu
 from jax.sharding import PartitionSpec as P
 
 SEQ = 128
+LANES = 128
+MESH = pl.DeviceIdType.MESH
 
 
 def passed_along(array, axis, by):
@@ -12,7 +18,7 @@
     return lax.ppermute(array, axis, pairs)
 
 
-def per_device(resid, enc_weight, enc_bias, dec_weight, dec_bias, lengths):
+def with_collectives(resid, enc_weight, enc_bias, dec_weight, dec_bias, lengths):
     valid = (jnp.arange(SEQ)[None, :] < lengths[:, None]).reshape(-1).astype(jnp.float32)
     pre = jnp.dot(resid[0], enc_weight[0], preferred_element_type=jnp.float32) + enc_bias[0]
     acts = (jax.nn.relu(pre) * valid[:, None]).astype(jnp.bfloat16)
@@ -20,7 +26,6 @@
     decoders = dec_weight[0]
     all_rows = lax.all_gather(acts, "dp", axis=0, tiled=True)
     initial = jnp.zeros((all_rows.shape[0], decoders.shape[2]), jnp.float32)
-    pieces = None
     pieces = [(all_rows, target)]
     current = all_rows
     for step in range(1, lax.axis_size("layer")):
@@ -36,6 +41,283 @@
         total = lax.cond((source >= 0) & (source <= target), apply_dec, lambda carry: carry, total)
     summed = lax.psum_scatter(total, "feat", scatter_dimension=1, tiled=True)
     return (summed + dec_bias[0][None, :]).astype(jnp.bfloat16)[None]
+
+
+def kernel(
+    n_feat, n_layer, blocks, rows, main, rem,
+    lengths_ref, resid_hbm, encw_hbm, encb_ref, decw_hbm, decb_ref,
+    out_ref,
+    resid, encw, decw, acts, acc, part, sbuf, from_low, from_high,
+    load_sem, dec_sem, acts_sem, dp_send, sib_send, far_send, relay_send, z_send, low_sem, high_sem,
+):
+    dp, layer, z = lax.axis_index("dp"), lax.axis_index("layer"), lax.axis_index("feat")
+    chunk = main + rem
+    packs = main // rem
+    tall = rows // packs
+    half = n_layer // 2
+    sibling = layer + 1 - 2 * (layer % 2)
+    own = blocks // 2
+
+    loads = [pltpu.make_async_copy(encw_hbm, encw, load_sem.at[0])]
+    for b in range(own):
+        span = pl.ds(b * rows, rows)
+        loads.append(pltpu.make_async_copy(resid_hbm.at[span], resid.at[span], load_sem.at[1 + b]))
+    for load in loads:
+        load.start()
+    dec_loads = [pltpu.make_async_copy(decw_hbm.at[s], decw.at[s], dec_sem.at[s]) for s in range(n_layer)]
+    for load in dec_loads:
+        load.start()
+
+    barrier = pltpu.get_barrier_semaphore()
+    partner = (layer + half) % n_layer
+    for where in ({"dp": 1 - dp}, {"layer": sibling}, {"layer": partner}):
+        pl.semaphore_signal(barrier, inc=1, device_id=where, device_id_type=MESH)
+
+    @pl.when(z > 0)
+    def _():
+        pl.semaphore_signal(barrier, inc=1, device_id={"feat": z - 1}, device_id_type=MESH)
+
+    @pl.when(z < n_feat - 1)
+    def _():
+        pl.semaphore_signal(barrier, inc=1, device_id={"feat": z + 1}, device_id_type=MESH)
+
+    ends = jnp.where(z == 0, 1, 0) + jnp.where(z == n_feat - 1, 1, 0)
+    pl.semaphore_wait(barrier, 5 - ends)
+
+    def block_of(i):
+        return (dp if i < own else 1 - dp) * own + i % own
+
+    def sent(source, i, sems, where):
+        block = block_of(i)
+        return pltpu.make_async_remote_copy(
+            src_ref=acts.at[source, block],
+            dst_ref=acts.at[source, block],
+            send_sem=sems.at[i],
+            recv_sem=acts_sem.at[source, block],
+            device_id=where,
+            device_id_type=MESH,
+        )
+
+    def dp_copy(i):
+        return sent(layer, i, dp_send, {"dp": 1 - dp})
+
+    def sib_copy(i):
+        return sent(layer, i, sib_send, {"layer": sibling})
+
+    def far_copy(i):
+        return sent(layer, i, far_send, {"layer": partner})
+
+    def relay_copy(i):
+        return sent(partner, i, relay_send, {"layer": sibling})
+
+    def arrived(source, i):
+        sent(source, i, dp_send, {"dp": 1 - dp}).wait_recv()
+
+    def spread(i):
+        @pl.when(layer < half)
+        def _():
+            far_copy(i).start()
+
+        @pl.when(layer % 2 == 0)
+        def _():
+            sib_copy(i).start()
+
+    def encode(i):
+        pre = jnp.dot(resid[i * rows : (i + 1) * rows], encw[...], preferred_element_type=jnp.float32)
+        pre = jnp.maximum(pre + encb_ref[...], 0.0)
+        for k in range(rows // SEQ):
+            length = lengths_ref[i * (rows // SEQ) + k]
+            piece = pre[k * SEQ : (k + 1) * SEQ]
+            position = lax.broadcasted_iota(jnp.int32, piece.shape, 0)
+            piece = jnp.where(position < length, piece, 0.0)
+            acts[layer, block_of(i), pl.ds(k * SEQ, SEQ), :] = piece.astype(jnp.bfloat16)
+        dp_copy(i).start()
+        spread(i)
+
+    def take(i):
+        arrived(layer, i)
+        spread(i)
+
+    def relay(i):
+        @pl.when(layer >= half)
+        def _():
+            arrived(layer - half, i)
+            relay_copy(i).start()
+
+    def z_copy(i, j, up):
+        landing, sems = (from_low, low_sem) if up else (from_high, high_sem)
+        return pltpu.make_async_remote_copy(
+            src_ref=sbuf.at[i, j],
+            dst_ref=landing.at[i, j],
+            send_sem=z_send.at[i, j],
+            recv_sem=sems.at[i, j],
+            device_id={"feat": z + 1 if up else z - 1},
+            device_id_type=MESH,
+        )
+
+    def decode(i):
+        block = block_of(i)
+        acc[...] = jnp.dot(acts[layer, block], decw[layer], preferred_element_type=jnp.float32)
+        for s in range(n_layer - 1):
+
+            @pl.when(s < layer)
+            def _():
+                @pl.when(s + half != layer)
+                def _():
+                    arrived(s, i)
+
+                acc[...] += jnp.dot(acts[s, block], decw[s], preferred_element_type=jnp.float32)
+
+        for j in range(n_feat):
+            first = j * chunk
+            part[i, j, 0:rows, :] = acc[:, first : first + main]
+            tail = acc[:, first + main : first + chunk]
+            part[i, j, rows : rows + tall, :] = jnp.concatenate(
+                [tail[k * tall : (k + 1) * tall] for k in range(packs)], axis=1
+            )
+
+        @pl.when(z == 0)
+        def _():
+            for j in reversed(range(1, n_feat)):
+                sbuf[i, j] = part[i, j].astype(jnp.bfloat16)
+                z_copy(i, j, True).start()
+
+        @pl.when(z == n_feat - 1)
+        def _():
+            for j in range(n_feat - 1):
+                sbuf[i, j] = part[i, j].astype(jnp.bfloat16)
+                z_copy(i, j, False).start()
+
+    def forward(i, j, up):
+        z_copy(i, j, up).wait_recv()
+        landing = from_low if up else from_high
+        sbuf[i, j] = (part[i, j] + landing[i, j].astype(jnp.float32)).astype(jnp.bfloat16)
+        z_copy(i, j, up).start()
+
+    def finish(i):
+        for place in range(1, n_feat - 1):
+
+            @pl.when(z == place)
+            def _():
+                ups = [(j, True) for j in reversed(range(place + 1, n_feat))]
+                downs = [(j, False) for j in range(place)]
+                order = ups + downs if len(ups) >= len(downs) else downs + ups
+                for j, up in order:
+                    forward(i, j, up)
+
+        @pl.when(z > 0)
+        def _():
+            z_copy(i, z, True).wait_recv()
+            part[i, z] += from_low[i, z].astype(jnp.float32)
+
+        @pl.when(z < n_feat - 1)
+        def _():
+            z_copy(i, z, False).wait_recv()
+            part[i, z] += from_high[i, z].astype(jnp.float32)
+
+        start = block_of(i) * rows
+        bias = decb_ref[...]
+        out_ref[pl.ds(start, rows), 0:main] = (part[i, z, 0:rows, :] + bias[:, 0:main]).astype(jnp.bfloat16)
+        tail = part[i, z, rows : rows + tall, :]
+        tail = jnp.concatenate([tail[:, k * rem : (k + 1) * rem] for k in range(packs)], axis=0)
+        out_ref[pl.ds(start, rows), main:chunk] = (tail + bias[:, main:chunk]).astype(jnp.bfloat16)
+
+    loads[0].wait()
+    for i in range(own):
+        loads[1 + i].wait()
+        encode(i)
+    relay(0)
+    for load in dec_loads:
+        load.wait()
+    decode(0)
+    for i in range(1, blocks):
+        if i == 1:
+            for later in range(own, blocks):
+                relay(1) if later == own else None
+                take(later)
+        else:
+            relay(i)
+        decode(i)
+        finish(i - 1)
+    finish(blocks - 1)
+
+    for i in range(blocks):
+        if i < own:
+            dp_copy(i).wait_send()
+
+        @pl.when(layer < half)
+        def _():
+            far_copy(i).wait_send()
+
+        @pl.when(layer % 2 == 0)
+        def _():
+            sib_copy(i).wait_send()
+
+        @pl.when(layer >= half)
+        def _():
+            relay_copy(i).wait_send()
+
+        for j in range(n_feat):
+
+            @pl.when(z != j)
+            def _():
+                z_copy(i, j, True).wait_send()
+
+
+def with_kernel(n_feat, n_layer, resid, enc_weight, enc_bias, dec_weight, dec_bias, lengths):
+    _, own_rows, width = resid.shape
+    feats = enc_weight.shape[2]
+    columns = dec_weight.shape[3]
+    chunk = columns // n_feat
+    main = chunk // LANES * LANES
+    rem = chunk - main
+    rows = own_rows // 2
+    blocks = 4
+    tall = rows // (main // rem)
+    packed = (blocks, n_feat, rows + tall, main)
+    anywhere = pl.BlockSpec(memory_space=pl.ANY)
+    vmem = pl.BlockSpec(memory_space=pltpu.VMEM)
+    dma = pltpu.SemaphoreType.DMA
+    out = pl.pallas_call(
+        functools.partial(kernel, n_feat, n_layer, blocks, rows, main, rem),
+        out_shape=jax.ShapeDtypeStruct((2 * own_rows, chunk), jnp.bfloat16),
+        in_specs=[pl.BlockSpec(memory_space=pltpu.SMEM), anywhere, anywhere, vmem, anywhere, vmem],
+        out_specs=vmem,
+        scratch_shapes=[
+            pltpu.VMEM((own_rows, width), jnp.bfloat16),
+            pltpu.VMEM((width, feats), jnp.bfloat16),
+            pltpu.VMEM((n_layer, feats, columns), jnp.bfloat16),
+            pltpu.VMEM((n_layer, blocks, rows, feats), jnp.bfloat16),
+            pltpu.VMEM((rows, columns), jnp.float32),
+            pltpu.VMEM(packed, jnp.float32),
+            pltpu.VMEM(packed, jnp.bfloat16),
+            pltpu.VMEM(packed, jnp.bfloat16),
+            pltpu.VMEM(packed, jnp.bfloat16),
+            dma((3,)),
+            dma((n_layer,)),
+            dma((n_layer, blocks)),
+            dma((blocks,)),
+            dma((blocks,)),
+            dma((blocks,)),
+            dma((blocks,)),
+            dma((blocks, n_feat)),
+            dma((blocks, n_feat)),
+            dma((blocks, n_feat)),
+        ],
+        compiler_params=pltpu.CompilerParams(
+            collective_id=0, has_side_effects=True, vmem_limit_bytes=56 * 2**20
+        ),
+    )(lengths, resid[0], enc_weight[0], enc_bias, dec_weight[0], dec_bias)
+    return out[None]
+
+
+def suits_kernel(sizes, resid, dec_weight):
+    chunk = dec_weight.shape[3] // (sizes["dp"] * sizes["feat"])
+    main, rem = chunk // LANES * LANES, chunk % LANES
+    rows = resid.shape[1] // (2 * sizes["dp"])
+    if sizes["dp"] != 2 or sizes["layer"] != 4 or sizes["feat"] < 2 or main == 0 or rem == 0:
+        return False
+    return main % rem == 0 and rows % SEQ == 0 and rows % (16 * (main // rem)) == 0
 
 
 def solution(mesh):
@@ -48,6 +330,13 @@
         P("dp"),
     )
     out_specs = P("layer", None, ("dp", "feat"))
-    return jax.shard_map(
-        per_device, mesh=mesh, in_specs=in_specs, out_specs=out_specs, check_vma=False
-    )
+    sizes = dict(mesh.shape)
+
+    def whole(resid, enc_weight, enc_bias, dec_weight, dec_bias, lengths):
+        body = with_collectives
+        if suits_kernel(sizes, resid, dec_weight):
+            body = functools.partial(with_kernel, sizes["feat"], sizes["layer"])
+        mapped = jax.shard_map(body, mesh=mesh, in_specs=in_specs, out_specs=out_specs, check_vma=False)
+        return mapped(resid, enc_weight, enc_bias, dec_weight, dec_bias, lengths)
+
+    return whole

time: 184 us -> 66.1 us (0.36)
  waiting for transfers between devices: 136 us -> 0 us
  Pallas kernels: 0 us -> 63.7 us
  matrix products: 22.2 us -> 0 us
  between operations: 13.5 us -> 0.01 us
  starting transfers between devices: 5.77 us -> 0 us
  other arithmetic: 3.11 us -> 0 us
    reduce_scatter x1 -> x0, waiting for transfers between devices: 84.8 us -> none  [per_device(): summed = lax.psum_scatter(total, 'feat', scatter_dimension=1, tiled=True)]
    pallas_call x0 -> x1, Pallas kernels: none -> 63.7 us  [with_kernel(): pl.pallas_call(functools.partial(kernel, n_feat, n_layer, blocks, rows, m...]
    ppermute x3 -> x0, waiting for transfers between devices: 28.7 us -> none  [passed_along(): return lax.ppermute(array, axis, pairs)]
    all_gather x1 -> x0, waiting for transfers between devices: 22.6 us -> none  [per_device(): all_rows = lax.all_gather(acts, 'dp', axis=0, tiled=True)]
    dot_general x4 -> x0, matrix products: 22.2 us -> none  [the longest x3 18.3 us: apply_dec(): return carry + jnp.dot(block, matrix, preferred_element_type=jnp.float32)]
    ppermute x3 -> x0, starting transfers between devices: 5.73 us -> none  [passed_along(): return lax.ppermute(array, axis, pairs)]
    broadcast_in_dim x1 -> x0, other arithmetic: 2.21 us -> none  [per_device(): return (summed + dec_bias[0][None, :]).astype(jnp.bfloat16)[None]]
    broadcast_in_dim x0 -> x1, local copies, waits for them, and re-layouts: none -> 2.2 us  [with_kernel(): return out[None]]
  transfers between devices with their start and end apart: 5 -> 0, of which waited for: 4 -> 0; matrix products, arithmetic and copies ran while one was open for 10% -> 0% of each run, Pallas kernels for 0% -> 0%
where the time goes in v1:
time: 66.1 us; the launch traced here: 65.9 us
  Pallas kernels  63.7 us (96%)
  local copies, waits for them, and re-layouts  2.2 us (3%)
    pallas_call x1, Pallas kernels, with_kernel(): pl.pallas_call(functools.partial(kernel, n_feat, n_layer, blocks, rows, m...  63.7 us
    broadcast_in_dim x1, local copies, waits for them, and re-layouts, with_kernel(): return out[None]  2.2 us

profile of v1, /device:TPU:4, one launch (start us, length us, event | category | flops | bytes accessed | tf_op | source)
XLA Modules:
  0.0 65.9 jit_solution(12532035552361529313)
XLA Ops:
  0.0 63.7 %shard_map.64 = bf16[1024,288]{1,0:T(8,128)(2,1)} custom-call(s32[4]{0:T(128)} %lengths_ref.1, bf16[512,2304]{1,0:T(8,128)(2,1)} %bitcast.6, bf16[2304,512]{1,0:T(8,128)(2,1)} %bitcast.7, f32[1,512]{1,0:T(1,128)} %encb_ref.1, bf16[4,512,1152]{2,1,0:T(8,128)(2,1)} %bitcast.4, f32[1,288]{1,0:T(1,128)} %decb_ref.1), custom_call_target="tpu_custom_call" | custom-call | tf_op jit(solution)/shard_map/pallas_call | solution.py:281
  63.7 2.2 %copy.7 = bf16[1,1024,288]{1,2,0:T(8,128)(2,1)} copy(bf16[1,1024,288]{2,1,0:T(8,128)(2,1)} %bitcast.5) | data formatting | bytes 1179648 | tf_op jit(solution)/shard_map/broadcast_in_dim | solution.py:311

commit v2 on v1

--- a/solution.py
+++ b/solution.py
@@ -9,6 +9,8 @@
 
 SEQ = 128
 LANES = 128
+BLOCKS = 8
+LAG = 3
 MESH = pl.DeviceIdType.MESH
 
 
@@ -65,8 +67,6 @@
     for load in loads:
         load.start()
     dec_loads = [pltpu.make_async_copy(decw_hbm.at[s], decw.at[s], dec_sem.at[s]) for s in range(n_layer)]
-    for load in dec_loads:
-        load.start()
 
     barrier = pltpu.get_barrier_semaphore()
     partner = (layer + half) % n_layer
@@ -194,7 +194,7 @@
         sbuf[i, j] = (part[i, j] + landing[i, j].astype(jnp.float32)).astype(jnp.bfloat16)
         z_copy(i, j, up).start()
 
-    def finish(i):
+    def pass_on(i):
         for place in range(1, n_feat - 1):
 
             @pl.when(z == place)
@@ -205,6 +205,7 @@
                 for j, up in order:
                     forward(i, j, up)
 
+    def finish(i):
         @pl.when(z > 0)
         def _():
             z_copy(i, z, True).wait_recv()
@@ -215,31 +216,37 @@
             z_copy(i, z, False).wait_recv()
             part[i, z] += from_high[i, z].astype(jnp.float32)
 
-        start = block_of(i) * rows
+        span = pl.ds(pl.multiple_of(block_of(i) * rows, rows), rows)
         bias = decb_ref[...]
-        out_ref[pl.ds(start, rows), 0:main] = (part[i, z, 0:rows, :] + bias[:, 0:main]).astype(jnp.bfloat16)
+        total = part[i, z, 0:rows, :] + bias[:, 0:main]
+        out_ref[0:main, span] = total.T.astype(jnp.bfloat16)
         tail = part[i, z, rows : rows + tall, :]
         tail = jnp.concatenate([tail[:, k * rem : (k + 1) * rem] for k in range(packs)], axis=0)
-        out_ref[pl.ds(start, rows), main:chunk] = (tail + bias[:, main:chunk]).astype(jnp.bfloat16)
+        tail = tail + bias[:, main:chunk]
+        out_ref[main:chunk, span] = tail.T.astype(jnp.bfloat16)
 
     loads[0].wait()
     for i in range(own):
         loads[1 + i].wait()
+        if i == 0:
+            for load in dec_loads:
+                load.start()
         encode(i)
-    relay(0)
-    for load in dec_loads:
-        load.wait()
-    decode(0)
-    for i in range(1, blocks):
-        if i == 1:
-            for later in range(own, blocks):
-                relay(1) if later == own else None
-                take(later)
-        else:
-            relay(i)
+    for i in range(blocks):
+        relay(i)
+        if 1 <= i <= own:
+            take(own + i - 1)
+        if i == 0:
+            for load in dec_loads:
+                load.wait()
         decode(i)
-        finish(i - 1)
-    finish(blocks - 1)
+        if i >= 1:
+            pass_on(i - 1)
+        if i >= LAG:
+            finish(i - LAG)
+    pass_on(blocks - 1)
+    for i in range(blocks - LAG, blocks):
+        finish(i)
 
     for i in range(blocks):
         if i < own:
@@ -271,8 +278,8 @@
     chunk = columns // n_feat
     main = chunk // LANES * LANES
     rem = chunk - main
-    rows = own_rows // 2
-    blocks = 4
+    blocks = BLOCKS
+    rows = 2 * own_rows // blocks
     tall = rows // (main // rem)
     packed = (blocks, n_feat, rows + tall, main)
     anywhere = pl.BlockSpec(memory_space=pl.ANY)
@@ -280,7 +287,7 @@
     dma = pltpu.SemaphoreType.DMA
     out = pl.pallas_call(
         functools.partial(kernel, n_feat, n_layer, blocks, rows, main, rem),
-        out_shape=jax.ShapeDtypeStruct((2 * own_rows, chunk), jnp.bfloat16),
+        out_shape=jax.ShapeDtypeStruct((chunk, 2 * own_rows), jnp.bfloat16),
         in_specs=[pl.BlockSpec(memory_space=pltpu.SMEM), anywhere, anywhere, vmem, anywhere, vmem],
         out_specs=vmem,
         scratch_shapes=[
@@ -293,7 +300,7 @@
             pltpu.VMEM(packed, jnp.bfloat16),
             pltpu.VMEM(packed, jnp.bfloat16),
             pltpu.VMEM(packed, jnp.bfloat16),
-            dma((3,)),
+            dma((1 + blocks // 2,)),
             dma((n_layer,)),
             dma((n_layer, blocks)),
             dma((blocks,)),
@@ -308,13 +315,13 @@
             collective_id=0, has_side_effects=True, vmem_limit_bytes=56 * 2**20
         ),
     )(lengths, resid[0], enc_weight[0], enc_bias, dec_weight[0], dec_bias)
-    return out[None]
+    return out.T[None]
 
 
 def suits_kernel(sizes, resid, dec_weight):
     chunk = dec_weight.shape[3] // (sizes["dp"] * sizes["feat"])
     main, rem = chunk // LANES * LANES, chunk % LANES
-    rows = resid.shape[1] // (2 * sizes["dp"])
+    rows = resid.shape[1] // BLOCKS
     if sizes["dp"] != 2 or sizes["layer"] != 4 or sizes["feat"] < 2 or main == 0 or rem == 0:
         return False
     return main % rem == 0 and rows % SEQ == 0 and rows % (16 * (main // rem)) == 0

time: 66.1 us -> 65.6 us (level)
    broadcast_in_dim x1 -> x0, local copies, waits for them, and re-layouts: 2.2 us -> none  [with_kernel(): return out[None]]
    unnamed x0 -> x1, local copies, waits for them, and re-layouts: none -> 1.92 us
where the time goes in v2:
time: 65.6 us; the launch traced here: 65.4 us
  Pallas kernels  63.5 us (97%)
  local copies, waits for them, and re-layouts  1.92 us (3%)
    pallas_call x1, Pallas kernels, with_kernel(): pl.pallas_call(functools.partial(kernel, n_feat, n_layer, blocks, rows, m...  63.5 us
    unnamed x1, local copies, waits for them, and re-layouts  1.92 us

profile of v2, /device:TPU:4, one launch (start us, length us, event | category | flops | bytes accessed | tf_op | source)
XLA Modules:
  0.0 65.4 jit_solution(15736496072949567430)
XLA Ops:
  0.0 63.5 %shard_map.64 = bf16[288,1024]{1,0:T(8,128)(2,1)} custom-call(s32[4]{0:T(128)} %lengths_ref.1, bf16[512,2304]{1,0:T(8,128)(2,1)} %bitcast.8, bf16[2304,512]{1,0:T(8,128)(2,1)} %bitcast.9, f32[1,512]{1,0:T(1,128)} %encb_ref.1, bf16[4,512,1152]{2,1,0:T(8,128)(2,1)} %bitcast.6, f32[1,288]{1,0:T(1,128)} %decb_ref.1), custom_call_target="tpu_custom_call" | custom-call | tf_op jit(solution)/shard_map/pallas_call | solution.py:288
  63.5 1.9 %copy.8 = bf16[1,1024,288]{1,2,0:T(8,128)(2,1)} copy(bf16[1,1024,288]{1,2,0:T(8,128)(2,1)} %bitcast.7) | data formatting | bytes 1179648

commit v3 on v2

--- a/solution.py
+++ b/solution.py
@@ -131,8 +131,8 @@
             position = lax.broadcasted_iota(jnp.int32, piece.shape, 0)
             piece = jnp.where(position < length, piece, 0.0)
             acts[layer, block_of(i), pl.ds(k * SEQ, SEQ), :] = piece.astype(jnp.bfloat16)
+        spread(i)
         dp_copy(i).start()
-        spread(i)
 
     def take(i):
         arrived(layer, i)
@@ -155,10 +155,21 @@
             device_id_type=MESH,
         )
 
+    def ahead(i):
+        if i + 1 < blocks:
+            relay(i + 1)
+        if i + 2 < own:
+            loads[3 + i].wait()
+            encode(i + 2)
+        if i < own:
+            take(own + i)
+
     def decode(i):
         block = block_of(i)
         acc[...] = jnp.dot(acts[layer, block], decw[layer], preferred_element_type=jnp.float32)
-        for s in range(n_layer - 1):
+        for s in reversed(range(n_layer - 1)):
+            if s == half - 1 and i == 0:
+                relay(0)
 
             @pl.when(s < layer)
             def _():
@@ -168,6 +179,7 @@
 
                 acc[...] += jnp.dot(acts[s, block], decw[s], preferred_element_type=jnp.float32)
 
+        ahead(i)
         for j in range(n_feat):
             first = j * chunk
             part[i, j, 0:rows, :] = acc[:, first : first + main]
@@ -226,19 +238,15 @@
         out_ref[main:chunk, span] = tail.T.astype(jnp.bfloat16)
 
     loads[0].wait()
-    for i in range(own):
-        loads[1 + i].wait()
-        if i == 0:
-            for load in dec_loads:
-                load.start()
-        encode(i)
+    loads[1].wait()
+    for load in dec_loads:
+        load.start()
+    encode(0)
+    loads[2].wait()
+    encode(1)
+    for load in dec_loads:
+        load.wait()
     for i in range(blocks):
-        relay(i)
-        if 1 <= i <= own:
-            take(own + i - 1)
-        if i == 0:
-            for load in dec_loads:
-                load.wait()
         decode(i)
         if i >= 1:
             pass_on(i - 1)

time: 65.6 us -> 61.5 us (0.938)
  Pallas kernels: 63.5 us -> 59.4 us
    pallas_call x1, Pallas kernels: 63.5 us -> 59.4 us  [with_kernel(): pl.pallas_call(functools.partial(kernel, n_feat, n_layer, blocks, rows, m...]
where the time goes in v3:
time: 61.5 us; the launch traced here: 61.4 us
  Pallas kernels  59.4 us (97%)
  local copies, waits for them, and re-layouts  1.92 us (3%)
    pallas_call x1, Pallas kernels, with_kernel(): pl.pallas_call(functools.partial(kernel, n_feat, n_layer, blocks, rows, m...  59.4 us
    unnamed x1, local copies, waits for them, and re-layouts  1.92 us

profile of v3, /device:TPU:4, one launch (start us, length us, event | category | flops | bytes accessed | tf_op | source)
XLA Modules:
  0.0 61.4 jit_solution(691062284199949921)
XLA Ops:
  0.0 59.4 %shard_map.64 = bf16[288,1024]{1,0:T(8,128)(2,1)} custom-call(s32[4]{0:T(128)} %lengths_ref.1, bf16[512,2304]{1,0:T(8,128)(2,1)} %bitcast.8, bf16[2304,512]{1,0:T(8,128)(2,1)} %bitcast.9, f32[1,512]{1,0:T(1,128)} %encb_ref.1, bf16[4,512,1152]{2,1,0:T(8,128)(2,1)} %bitcast.6, f32[1,288]{1,0:T(1,128)} %decb_ref.1), custom_call_target="tpu_custom_call" | custom-call | tf_op jit(solution)/shard_map/pallas_call | solution.py:296
  59.4 1.9 %copy.8 = bf16[1,1024,288]{1,2,0:T(8,128)(2,1)} copy(bf16[1,1024,288]{1,2,0:T(8,128)(2,1)} %bitcast.7) | data formatting | bytes 1179648
